TPU v7x, 512 devices: a whole 4x8x8 slice. The times are simulated.
512 devices in a mesh: node: 128 (over y, z, core), rep: 4 (over x).
Axes of the slice: x: 4, y: 8, z: 8, core: 2. Of those that a mesh axis runs over, the one named last changes fastest.
Arguments:
- history_in: bfloat16 [262144, 128], P('node'), may hold values from 0 to 2
- history_mid: bfloat16 [262144, 128], P('node'), may hold values from 0 to 2
- current: bfloat16 [131072, 128], P(('node', 'rep')), may hold values from 0 to 2
- initial: bfloat16 [131072, 128], P(('node', 'rep')), may hold values from 0 to 2
- batch_rows: int32 [131072], P(('node', 'rep')), may hold values from 0 to 2047, as said below
- halo_rows: int32 [512, 128, 8], P(('node', 'rep')), may hold values from 0 to 2047
- halo_count: int32 [512, 128], P(('node', 'rep')), may hold values from 1 to 8, as said below
- adj_cols: int32 [512, 2, 8], P(('node', 'rep')), may hold values from 0 to 9, as said below
- adj_vals: bfloat16 [512, 2, 8, 128, 128], P(('node', 'rep')), may hold values from -0.1875 to 0.1875
- upstream: bfloat16 [131072, 128], P(('node', 'rep')), may hold values from -6 to 6
- weight_a: bfloat16 [128, 128], replicated, may hold values from -0.5 to 0.5
- weight_b: bfloat16 [128, 128], replicated, may hold values from -0.5 to 0.5
Outputs:
- final_out: bfloat16 [131072, 128], P(('node', 'rep'))
- history_in_new: bfloat16 [262144, 128], P('node')
- history_mid_new: bfloat16 [262144, 128], P('node')
- grad_a: float32 [128, 128], replicated
- grad_b: float32 [128, 128], replicated
Inputs may be any that keep to these rules, and one draw needn't show every extreme that they name: `batch_rows`: for each index of node the 4 replicas' batch rows are distinct and cover half of the shard. `halo_count`: every count is at least 1; each device has an owner with all 8 slots live, and some owner has all 8 slots live from every device. `adj_cols`: each row block r names its own batch tile r among its 8 tiles; every halo tile is named by some row block.
All inputs are finite; a program needn't handle non-finite values.
Results may differ from a plain program's by a relative error of at most 0.011.
The roundings to bfloat16 on the way count: a program that leaves them out, or rounds other values in their place, can miss the bound.
Values may be sent and summed in bfloat16 or wider, within the bound.
A program may use at most 64 MiB of HBM per device.

v0:
```python
import math

import jax
import jax.numpy as jnp
from jax import lax
from jax.sharding import PartitionSpec as P

alpha_mix = 0.1
beta_first = math.log(1.0 + 0.5 / 3.0)
beta_second = math.log(1.0 + 0.5 / 4.0)


def gcn_layer(feature_tiles, columns, edge_tiles, initial_rows, weight, beta_rate):
    picked = jnp.take(feature_tiles, columns, axis=0)
    aggregate = jnp.einsum("rkij,rkjh->rih", edge_tiles, picked, preferred_element_type=jnp.float32)
    aggregate = aggregate.reshape(-1, aggregate.shape[-1])
    support = ((1.0 - alpha_mix) * aggregate + alpha_mix * initial_rows.astype(jnp.float32)).astype(
        jnp.bfloat16
    )
    preact = (1.0 - beta_rate) * support.astype(jnp.float32) + beta_rate * jnp.dot(
        support, weight, preferred_element_type=jnp.float32
    )
    return (support, preact, jnp.maximum(preact, 0.0).astype(jnp.bfloat16))


def on_device(
    history_in,
    history_mid,
    current,
    initial,
    batch_rows,
    halo_rows,
    halo_count,
    adj_cols,
    adj_vals,
    upstream,
    weight_a,
    weight_b,
):
    owner_rows = halo_rows[0]
    counts = halo_count[0]
    columns = adj_cols[0]
    edge_tiles = adj_vals[0]
    blocks = columns.shape[0]
    tile_size = edge_tiles.shape[2]
    hidden_size = current.shape[1]
    asked_rows = lax.all_to_all(owner_rows, "node", split_axis=0, concat_axis=0, tiled=True)
    live_mask = (lax.broadcasted_iota(jnp.int32, owner_rows.shape, 1) < counts[:, None])[:, :, None]
    nothing = jnp.zeros((), jnp.bfloat16)

    def as_tiles(received):
        return jnp.where(live_mask, received, nothing).reshape(-1, tile_size, hidden_size)

    halo_a = lax.all_to_all(
        jnp.take(history_in, asked_rows, axis=0), "node", split_axis=0, concat_axis=0, tiled=True
    )
    tiles_a = jnp.concatenate(
        [current.reshape(blocks, tile_size, hidden_size), as_tiles(halo_a)], 0
    )
    support_a, preact_a, fresh_a = gcn_layer(
        tiles_a, columns, edge_tiles, initial, weight_a, beta_first
    )
    halo_b = lax.all_to_all(
        jnp.take(history_mid, asked_rows, axis=0), "node", split_axis=0, concat_axis=0, tiled=True
    )
    tiles_b = jnp.concatenate(
        [fresh_a.reshape(blocks, tile_size, hidden_size), as_tiles(halo_b)], 0
    )
    support_b, preact_b, final_rows = gcn_layer(
        tiles_b, columns, edge_tiles, initial, weight_b, beta_second
    )
    all_rows, all_current, all_fresh = (
        lax.all_gather(batch_rows, "rep", axis=0, tiled=True),
        lax.all_gather(current, "rep", axis=0, tiled=True),
        lax.all_gather(fresh_a, "rep", axis=0, tiled=True),
    )
    history_in_new = history_in.at[all_rows].set(all_current)
    history_mid_new = history_mid.at[all_rows].set(all_fresh)
    rows_total = current.shape[0] * lax.axis_size("node") * lax.axis_size("rep")
    scale = 1.0 / math.sqrt(rows_total)
    gated_b = jnp.where(preact_b > 0, upstream.astype(jnp.float32), 0.0).astype(jnp.bfloat16)
    part_b = beta_second * jnp.dot(support_b.T, gated_b, preferred_element_type=jnp.float32)
    support_grad = (1.0 - beta_second) * gated_b.astype(jnp.float32) + beta_second * jnp.dot(
        gated_b, weight_b.T, preferred_element_type=jnp.float32
    )
    agg_grad = ((1.0 - alpha_mix) * support_grad).astype(jnp.bfloat16)
    contrib = jnp.einsum(
        "rkij,rih->rkjh",
        edge_tiles,
        agg_grad.reshape(blocks, tile_size, hidden_size),
        preferred_element_type=jnp.float32,
    )
    onehot = (columns[:, :, None] == lax.broadcasted_iota(jnp.int32, (1, 1, blocks), 2)).astype(
        jnp.float32
    )
    fresh_grad = jnp.einsum("rkc,rkjh->cjh", onehot, contrib, precision=lax.Precision.HIGHEST)
    fresh_grad = fresh_grad.reshape(-1, hidden_size)
    gated_a = jnp.where(preact_a > 0, fresh_grad, 0.0).astype(jnp.bfloat16)
    part_a = beta_first * jnp.dot(support_a.T, gated_a, preferred_element_type=jnp.float32)
    grad_a, grad_b = lax.psum((part_a, part_b), ("node", "rep"))
    return (final_rows, history_in_new, history_mid_new, grad_a * scale, grad_b * scale)


def solution(mesh):
    in_specs = (
        P("node", None),
        P("node", None),
        P(("node", "rep"), None),
        P(("node", "rep"), None),
        P(("node", "rep")),
        P(("node", "rep"), None, None),
        P(("node", "rep"), None),
        P(("node", "rep"), None, None),
        P(("node", "rep"), None, None, None, None),
        P(("node", "rep"), None),
        P(),
        P(),
    )
    out_specs = (P(("node", "rep"), None), P("node", None), P("node", None), P(), P())
    return jax.shard_map(
        on_device, mesh=mesh, in_specs=in_specs, out_specs=out_specs, check_vma=False
    )
```

profile of v0, /device:TPU:1, one launch (start us, length us, event | category | flops | bytes accessed | tf_op | source)
XLA Modules:
  0.0 372.5 jit_solution(6197121180927234337)
XLA Ops:
  7.2 1.1 copy.37
  8.4 0.6 copy-done.10
  9.2 29.7 %all_to_all.22 = s32[128,1,8]{2,1,0:T(1,128)S(1)} all-to-all(s32[128,1,8]{2,1,0:T(1,128)S(1)} %bitcast.83), channel_id=1, replica_groups=mesh['node'=128,'rep'=4] {'node'}, dimensions={0} | all-to-all | bytes 8192 | tf_op jit(solution)/shard_map/all_to_all | solution.py:47
  39.1 3.2 gather_fusion
  42.3 3.2 gather_fusion.2
  45.5 1.0 bitcast_select_fusion.1
  46.5 5.9 %all-to-all-start.1 = ((bf16[128,8,128]{2,1,0:T(8,128)(2,1)}), bf16[128,8,128]{2,1,0:T(8,128)(2,1)S(1)}, u32[]{:S(2)}, u32[]{:S(2)}) async-start(bf16[128,8,128]{2,1,0:T(8,128)(2,1)} %get-tuple-element.11), calls=%async_computation.1 | async-start | bytes 524288 | tf_op jit(solution)/shard_map/all_to_all | solution.py:54
  52.9 0.7 copy-done.11
  53.6 8.3 %all-gather = s32[4,1,256]{2,1,0:T(1,128)S(1)} all-gather(s32[1,1,256]{2,1,0:T(1,128)S(1)} %bitcast.86), channel_id=1, replica_groups=mesh['node'=128,'rep'=4] {'rep'}, dimensions={0}, use_global_device_ids=true | all-gather | bytes 5120 | tf_op jit(solution)/shard_map/all_gather | solution.py:73
  61.9 4.8 %all-to-all-done.1 = bf16[128,8,128]{2,1,0:T(8,128)(2,1)S(1)} async-done(((bf16[128,8,128]{2,1,0:T(8,128)(2,1)}), bf16[128,8,128]{2,1,0:T(8,128)(2,1)S(1)}, u32[]{:S(2)}, u32[]{:S(2)}) %all-to-all-start.1) | async-done | bytes 262176 | tf_op jit(solution)/shard_map/all_to_all | solution.py:54
  66.7 10.6 %all-to-all-start.2 = ((bf16[128,8,128]{2,1,0:T(8,128)(2,1)}), bf16[128,8,128]{2,1,0:T(8,128)(2,1)S(1)}, u32[]{:S(2)}, u32[]{:S(2)}) async-start(bf16[128,8,128]{2,1,0:T(8,128)(2,1)} %get-tuple-element.12), calls=%async_computation.2 | async-start | bytes 524288 | tf_op jit(solution)/shard_map/all_to_all | solution.py:63
  77.4 10.3 %all_gather.10 = bf16[1024,128]{1,0:T(8,128)(2,1)S(1)} all-gather(bf16[256,128]{1,0:T(8,128)(2,1)S(1)} %copy-done.5), channel_id=1, replica_groups=mesh['node'=128,'rep'=4] {'rep'}, dimensions={0}, use_global_device_ids=true | all-gather | bytes 327680 | tf_op jit(solution)/shard_map/all_gather | solution.py:74
  87.6 0.7 copy-done.12
  88.4 3.5 scatter_fusion
  92.7 0.6 gather_fusion.1
  94.2 0.7 copy-done.8
  95.1 0.6 gather_fusion.3
  96.2 0.8 maximum_convert_fusion
  97.1 0.8 convolution_multiply_fusion.3
  99.0 0.8 convolution_multiply_fusion.4
  99.8 10.1 %all_gather.11 = bf16[1024,128]{1,0:T(8,128)(2,1)S(1)} all-gather(bf16[256,128]{1,0:T(8,128)(2,1)S(1)} %get-tuple-element.13), channel_id=1, replica_groups=mesh['node'=128,'rep'=4] {'rep'}, dimensions={0}, use_global_device_ids=true | all-gather | bytes 327680 | tf_op jit(solution)/shard_map/all_gather | solution.py:75
  110.0 3.5 scatter_fusion.1
  113.4 250.7 %all-reduce.3.cloned.1.call-done = (f32[128,128]{1,0:T(8,128)}, f32[128,128]{1,0:T(8,128)}) async-done(((f32[128,128]{1,0:T(8,128)}, f32[128,128]{1,0:T(8,128)}), (f32[128,128]{1,0:T(8,128)}, f32[128,128]{1,0:T(8,128)})) %all-reduce.3.cloned.1.call-update) | async-done | bytes 131088 | tf_op jit(solution)/shard_map/psum | solution.py:100
  364.1 1.5 broadcast_multiply_fusion
  (51 shorter events, 4.4 us)
Async XLA Ops:
  7.2 89.0 %copy-start = (bf16[128,128]{1,0:T(8,128)(2,1)S(1)}, bf16[128,128]{1,0:T(8,128)(2,1)}, u32[]{:S(2)}) copy-start(bf16[128,128]{1,0:T(8,128)(2,1)} %param.27) | copy-start | bytes 98308
  7.2 1.2 copy-start.3
  8.4 0.7 copy-start.10
  46.5 6.0 %copy-start.4 = (bf16[1,2,8,128,128]{4,3,2,1,0:T(8,128)(2,1)S(1)}, bf16[1,2,8,128,128]{4,3,2,1,0:T(8,128)(2,1)}, u32[]{:S(2)}) copy-start(bf16[1,2,8,128,128]{4,3,2,1,0:T(8,128)(2,1)} %param.24) | copy-start | bytes 1572868
  46.5 5.9 %copy-start.9 = (s32[1,2,8]{2,1,0:T(2,128)S(1)}, s32[1,2,8]{2,1,0:T(2,128)}, u32[]{:S(2)}) copy-start(s32[1,2,8]{2,1,0:T(2,128)} %param.23) | copy-start | bytes 196
  46.5 20.2 %all-to-all-start.1 = ((bf16[128,8,128]{2,1,0:T(8,128)(2,1)}), bf16[128,8,128]{2,1,0:T(8,128)(2,1)S(1)}, u32[]{:S(2)}, u32[]{:S(2)}) async-start(bf16[128,8,128]{2,1,0:T(8,128)(2,1)} %get-tuple-element.11), calls=%async_computation.1 | async-start | bytes 524288 | tf_op jit(solution)/shard_map/all_to_all | solution.py:54
  52.9 0.7 copy-start.11
  66.7 10.7 %copy-start.5 = (bf16[256,128]{1,0:T(8,128)(2,1)S(1)}, bf16[256,128]{1,0:T(8,128)(2,1)}, u32[]{:S(2)}) copy-start(bf16[256,128]{1,0:T(8,128)(2,1)} %param.18) | copy-start | bytes 196612
  66.7 25.2 %all-to-all-start.2 = ((bf16[128,8,128]{2,1,0:T(8,128)(2,1)}), bf16[128,8,128]{2,1,0:T(8,128)(2,1)S(1)}, u32[]{:S(2)}, u32[]{:S(2)}) async-start(bf16[128,8,128]{2,1,0:T(8,128)(2,1)} %get-tuple-element.12), calls=%async_computation.2 | async-start | bytes 524288 | tf_op jit(solution)/shard_map/all_to_all | solution.py:63
  77.3 286.8 %all-reduce.3.cloned.1.call-start = ((), (), s32[]{:S(2)}) async-start(), calls=%async_computation.3 | async-start | bytes 262144 | tf_op jit(solution)/shard_map/psum | solution.py:100
  87.6 0.7 copy-start.12
  91.9 0.8 copy-start.2
  93.3 0.8 copy-start.6
  94.2 0.8 copy-start.8
  96.2 0.8 copy-start.7
  113.4 252.2 %copy-start.1 = (bf16[2048,128]{1,0:T(8,128)(2,1)}, bf16[2048,128]{1,0:T(8,128)(2,1)S(1)}, u32[]{:S(2)}) copy-start(bf16[2048,128]{1,0:T(8,128)(2,1)S(1)} %scatter_fusion.1) | copy-start | bytes 1572868
Sparse Core Ops, SparseCore 0:
  99.9 264.1 all-reduce.2
where the time goes:
time: 373 us; the launch traced here: 372 us
  waiting for transfers between devices  256 us (69%)
  blocking collectives  58.4 us (16%)
  local copies, waits for them, and re-layouts  20.4 us (5%)
  starting transfers between devices  16.5 us (4%)
  between operations  14.3 us (4%)
  matrix products  4.32 us (1%)
    psum x1, waiting for transfers between devices, on_device(): grad_a, grad_b = lax.psum((part_a, part_b), ('node', 'rep'))  251 us
    all_to_all x1, blocking collectives, on_device(): lax.all_to_all(owner_rows, 'node', split_axis=0, concat_axis=0, tiled=True)  29.7 us
    all_to_all x1, starting transfers between devices, on_device(): lax.all_to_all(jnp.take(history_mid, asked_rows, axis=0), 'node', split_a...  10.6 us
    all_gather x1, blocking collectives, on_device(): lax.all_gather(current, 'rep', axis=0, tiled=True)  10.3 us
    all_gather x1, blocking collectives, on_device(): lax.all_gather(fresh_a, 'rep', axis=0, tiled=True)  10.1 us
    all_gather x1, blocking collectives, on_device(): lax.all_gather(batch_rows, 'rep', axis=0, tiled=True)  8.28 us
  transfers between devices with their start and end apart: 3, of which 2 were waited for; matrix products, arithmetic and copies ran while one was open for 2% of the time, Pallas kernels for 0%

commit v1 on v0

v1 whole, which is shorter than its diff:
```python
import functools
import math

import jax
import jax.numpy as jnp
from jax import lax
from jax.experimental import pallas as pl
from jax.experimental.pallas import tpu as pltpu
from jax.sharding import PartitionSpec as P

ALPHA = 0.1
BETA_A = math.log(1.0 + 0.5 / 3.0)
BETA_B = math.log(1.0 + 0.5 / 4.0)
MESH = pl.DeviceIdType.MESH
F32 = jnp.float32
BF16 = jnp.bfloat16

NY = 8
NW = 16
NX = 4
CAP = 8
TILE = 128
H = 128
BATCH = 256
SHARD = 2048
RB = 2
NB = 8
W_ORDER = (8, 7, 9, 6, 10, 5, 11, 4, 12, 3, 13, 2, 14, 1, 15, 0)
CHUNK = 4
ROWS = NY * CAP * CHUNK
PARTS = 8
BLOCK = SHARD // PARTS


def fill(ref, sem):
    pltpu.make_async_copy(ref, ref, sem).wait()


def dot(lhs, rhs):
    return jnp.dot(lhs, rhs, preferred_element_type=F32)


def dot_t(lhs, rhs):
    return lax.dot_general(lhs, rhs, (((0,), (0,)), ((), ())), preferred_element_type=F32)


def kernel(
    halo_rows,
    halo_count,
    batch_rows,
    cols,
    hist_in,
    hist_mid,
    current,
    initial,
    upstream,
    adj,
    weight_a,
    weight_b,
    final_out,
    new_in,
    new_mid,
    grad_a,
    grad_b,
    asked_y,
    asked_t,
    ask_row,
    asked_w,
    hist,
    onehot,
    rows_out,
    halo,
    tiles,
    adj_v,
    cur_all,
    fresh_all,
    br_all,
    refresh,
    base_mid,
    init_v,
    up_v,
    wa_v,
    wb_v,
    f_fwd,
    f_bwd,
    part,
    sum_w,
    sum_y,
    sum_x,
    total,
    load_sem,
    y_sem,
    w_sem,
    h_send,
    h_recv,
    rep_sem,
    red_sem,
    ready,
):
    node, x = lax.axis_index("node"), lax.axis_index("rep")
    y, w = node // NW, node % NW

    def dev(yy, ww, xx):
        return (yy * NW + ww, xx)

    def send(src, dst, s_sem, r_sem, device):
        pltpu.make_async_remote_copy(
            src_ref=src, dst_ref=dst, send_sem=s_sem, recv_sem=r_sem, device_id=device, device_id_type=MESH
        ).start()

    loads = [
        (hist_in, hist.at[:, pl.ds(0, H)]),
        (hist_mid, hist.at[:, pl.ds(H, H)]),
        (current, cur_all.at[x]),
        (adj, adj_v),
        (initial, init_v),
        (upstream, up_v),
        (weight_a, wa_v),
        (weight_b, wb_v),
    ]
    copies = [pltpu.make_async_copy(s, d, load_sem.at[i]) for i, (s, d) in enumerate(loads)]
    for c in copies:
        c.start()

    barrier = pltpu.get_barrier_semaphore()
    for k in range(1, NY):
        pl.semaphore_signal(barrier, inc=1, device_id=dev((y + k) % NY, w, x), device_id_type=MESH)
    for k in range(1, NW):
        pl.semaphore_signal(barrier, inc=1, device_id=dev(y, (w + k) % NW, x), device_id_type=MESH)
    for k in range(1, NX):
        pl.semaphore_signal(barrier, inc=1, device_id=dev(y, w, (x + k) % NX), device_id_type=MESH)

    slot = lax.broadcasted_iota(jnp.int32, (CAP, NY * NW), 0)
    asked_y[y] = jnp.where(slot < halo_count[...], halo_rows[...], -1)
    br_all[x] = batch_rows[...]
    pl.semaphore_wait(barrier, NY + NW + NX - 3)

    for k in range(1, NY):
        send(asked_y.at[y], asked_y.at[y], y_sem.at[0], y_sem.at[1], dev((y + k) % NY, w, x))
    fill(asked_y.at[pl.ds(0, NY - 1)], y_sem.at[1])
    lists = asked_y[...].reshape(NY * CAP, NY * NW)
    lists = jnp.concatenate([lists, jnp.zeros((128 - NY * CAP, NY * NW), jnp.int32)], 0)
    asked_t[...] = lists.T
    mine = asked_t[pl.ds(pl.multiple_of(y * NW, NW), NW), :]
    for i in range(NW):
        ask_row[i] = mine[i : i + 1, :]
    for i, k in enumerate(W_ORDER):
        if k:
            to = (w + k) % NW
            send(ask_row.at[to], asked_w.at[i], w_sem.at[0], w_sem.at[1], dev(y, to, x))
    asked_w[NW - 1] = ask_row[w]

    copies[2].wait()
    for k in range(1, NX):
        to = dev(y, w, (x + k) % NX)
        send(br_all.at[x], br_all.at[x], rep_sem.at[0], rep_sem.at[1], to)
        send(cur_all.at[x], cur_all.at[x], rep_sem.at[2], rep_sem.at[3], to)

    fill(asked_w.at[pl.ds(0, NW - 1)], w_sem.at[1])
    wanted = jnp.concatenate([asked_w[i] for i in range(NW)] + [jnp.zeros((128 - NW, 128), jnp.int32)], 0)
    asked_t[...] = wanted.T
    wanted = asked_t[pl.ds(0, NY * CAP), :]
    lane = lax.broadcasted_iota(jnp.int32, (NY * CAP, SHARD), 1)
    for c in range(NW // CHUNK):
        for q in range(CHUNK):
            i = c * CHUNK + q
            hit = jnp.broadcast_to(wanted[:, i : i + 1], (NY * CAP, SHARD)) == lane
            onehot[pl.ds(q * NY * CAP, NY * CAP), :] = hit.astype(F32).astype(BF16)
        if c == 0:
            copies[0].wait()
            copies[1].wait()
        got = dot(onehot[...], hist[...])
        both = jnp.concatenate(
            [got[:, :H].reshape(CHUNK * NY, CAP, H), got[:, H:].reshape(CHUNK * NY, CAP, H)], 1
        )
        rows_out[pl.ds(c * CHUNK, CHUNK)] = both.astype(BF16).reshape(CHUNK, NY, 2 * CAP, H)
        for q in range(CHUNK):
            i = c * CHUNK + q
            k = W_ORDER[i]
            to_w = (w + NW - k) % NW

            def reply(ky, carry, i=i, to_w=to_w):
                to_y = (y + ky) % NY
                send(rows_out.at[i, to_y], halo.at[y, w], h_send, h_recv.at[y], dev(to_y, to_w, x))
                return carry

            lax.fori_loop(0 if k else 1, NY, reply, 0)
    halo[y, w] = rows_out[NW - 1, y]

    copies[3].wait()
    for r in range(RB):
        for c in range(RB):
            acc = jnp.zeros((TILE, TILE), F32)
            for k in range(NB):
                acc = acc + jnp.where(cols[r, k] == c, adj_v[r, k].astype(F32), 0.0)
            high = acc.astype(BF16)
            low = (acc - high.astype(F32)).astype(BF16)
            rs, cs = pl.ds(r * TILE, TILE), pl.ds(c * TILE, TILE)
            f_fwd[rs, cs] = high
            f_fwd[rs, pl.ds(BATCH + c * TILE, TILE)] = low
            acc_t = acc.T
            high_t = acc_t.astype(BF16)
            f_bwd[cs, rs] = high_t
            f_bwd[cs, pl.ds(BATCH + r * TILE, TILE)] = (acc_t - high_t.astype(F32)).astype(BF16)
    for c in range(RB):
        tiles[c, :, pl.ds(0, H)] = cur_all[x, pl.ds(c * TILE, TILE), :]
        tiles[c, :, pl.ds(H, H)] = jnp.zeros((TILE, H), BF16)

    fill(br_all.at[pl.ds(0, NX - 1)], rep_sem.at[1])
    fill(cur_all.at[pl.ds(0, NX - 1)], rep_sem.at[3])
    for p in range(PARTS):
        rows = pl.ds(p * BLOCK, BLOCK)
        row = p * BLOCK + lax.broadcasted_iota(jnp.int32, (BLOCK, BATCH), 0)
        for r in range(NX):
            refresh[rows, pl.ds(r * BATCH, BATCH)] = (br_all[r] == row).astype(F32).astype(BF16)
    new_rows = jnp.concatenate([cur_all[...].reshape(NX * BATCH, H), jnp.ones((NX * BATCH, H), BF16)], 1)
    for p in range(PARTS):
        rows = pl.ds(p * BLOCK, BLOCK)
        put = dot(refresh[rows, :], new_rows)
        kept = put[:, H:] == 0.0
        new_in[rows, :] = jnp.where(kept, hist[rows, pl.ds(0, H)].astype(F32), put[:, :H]).astype(BF16)
        base_mid[rows, :] = jnp.where(kept, hist[rows, pl.ds(H, H)].astype(F32), 0.0).astype(BF16)
    for c in copies[4:]:
        c.wait()

    for k in range(NY):
        yy = (y + k) % NY
        if k:
            fill(halo.at[yy], h_recv.at[yy])
        else:
            fill(halo.at[y, pl.ds(0, NW - 1)], h_recv.at[y])
        block = halo[yy].astype(F32)
        pair = [block[:, :CAP, :].reshape(TILE, H), block[:, CAP:, :].reshape(TILE, H)]
        tiles[RB + yy] = jnp.concatenate(pair, 1).astype(BF16)
    for k in range(1, NX):
        pl.semaphore_signal(ready, inc=1, device_id=dev(y, w, (x + k) % NX), device_id_type=MESH)

    sums = []
    for r in range(RB):
        left = jnp.concatenate([adj_v[r, k] for k in range(NB)], 1)
        right = jnp.concatenate([tiles[cols[r, k]] for k in range(NB)], 0)
        sums.append(dot(left, right))
    agg = jnp.concatenate(sums, 0)
    init = ALPHA * init_v[...].astype(F32)
    support_a = ((1.0 - ALPHA) * agg[:, :H] + init).astype(BF16)
    preact_a = (1.0 - BETA_A) * support_a.astype(F32) + BETA_A * dot(support_a, wa_v[...])
    fresh = jnp.maximum(preact_a, 0.0).astype(BF16)
    fresh_all[x] = fresh
    for k in range(1, NX):
        send(fresh_all.at[x], fresh_all.at[x], rep_sem.at[4], rep_sem.at[5], dev(y, w, (x + k) % NX))
    agg_b = agg[:, H:] + dot(f_fwd[...], jnp.concatenate([fresh, fresh], 0))
    support_b = ((1.0 - ALPHA) * agg_b + init).astype(BF16)
    preact_b = (1.0 - BETA_B) * support_b.astype(F32) + BETA_B * dot(support_b, wb_v[...])
    final_out[...] = jnp.maximum(preact_b, 0.0).astype(BF16)
    gated_b = jnp.where(preact_b > 0, up_v[...].astype(F32), 0.0).astype(BF16)
    part[pl.ds(H, H), :] = BETA_B * dot_t(support_b, gated_b)
    back = lax.dot_general(gated_b, wb_v[...], (((1,), (1,)), ((), ())), preferred_element_type=F32)
    support_grad = (1.0 - BETA_B) * gated_b.astype(F32) + BETA_B * back
    agg_grad = ((1.0 - ALPHA) * support_grad).astype(BF16)
    fresh_grad = dot(f_bwd[...], jnp.concatenate([agg_grad, agg_grad], 0))
    gated_a = jnp.where(preact_a > 0, fresh_grad, 0.0).astype(BF16)
    part[pl.ds(0, H), :] = BETA_A * dot_t(support_a, gated_a)

    piece = 2 * H // NW
    for k in W_ORDER[:-1]:
        to = (w + k) % NW
        rows = pl.ds(pl.multiple_of(to * piece, piece), piece)
        send(part.at[rows, :], sum_w.at[w], red_sem.at[0], red_sem.at[1], dev(y, to, x))
    sum_w[w] = part[pl.ds(pl.multiple_of(w * piece, piece), piece), :]
    fill(sum_w.at[pl.ds(0, NW - 1)], red_sem.at[1])
    sum_y[y] = jnp.sum(sum_w[...], 0)
    for k in range(1, NY):
        send(sum_y.at[y], sum_y.at[y], red_sem.at[2], red_sem.at[3], dev((y + k) % NY, w, x))
    fill(sum_y.at[pl.ds(0, NY - 1)], red_sem.at[3])
    sum_x[x] = jnp.sum(sum_y[...], 0)
    for k in range(1, NX):
        send(sum_x.at[x], sum_x.at[x], red_sem.at[4], red_sem.at[5], dev(y, w, (x + k) % NX))
    fill(sum_x.at[pl.ds(0, NX - 1)], red_sem.at[5])
    total[w] = jnp.sum(sum_x[...], 0) * (1.0 / math.sqrt(NY * NW * NX * BATCH))
    for k in W_ORDER[:-1]:
        send(total.at[w], total.at[w], red_sem.at[6], red_sem.at[7], dev(y, (w + k) % NW, x))

    pl.semaphore_wait(ready, NX - 1)
    fill(fresh_all.at[pl.ds(0, NX - 1)], rep_sem.at[5])
    fresh_rows = fresh_all[...].reshape(NX * BATCH, H)
    for p in range(PARTS):
        rows = pl.ds(p * BLOCK, BLOCK)
        put = dot(refresh[rows, :], fresh_rows)
        new_mid[rows, :] = (put + base_mid[rows, :].astype(F32)).astype(BF16)

    fill(total.at[pl.ds(0, NW - 1)], red_sem.at[7])
    half = NW // 2
    grad_a[...] = total[pl.ds(0, half)].reshape(H, H)
    grad_b[...] = total[pl.ds(half, half)].reshape(H, H)

    fill(asked_y.at[pl.ds(0, NY - 1)], y_sem.at[0])
    fill(asked_w.at[pl.ds(0, NW - 1)], w_sem.at[0])
    fill(br_all.at[pl.ds(0, NX - 1)], rep_sem.at[0])
    fill(cur_all.at[pl.ds(0, NX - 1)], rep_sem.at[2])
    fill(fresh_all.at[pl.ds(0, NX - 1)], rep_sem.at[4])
    for k in range(NY):
        fill(halo.at[k] if k else halo.at[k, pl.ds(0, NW - 1)], h_send)
    fill(sum_w.at[pl.ds(0, NW - 1)], red_sem.at[0])
    fill(sum_y.at[pl.ds(0, NY - 1)], red_sem.at[2])
    fill(sum_x.at[pl.ds(0, NX - 1)], red_sem.at[4])
    fill(total.at[pl.ds(0, NW - 1)], red_sem.at[6])


def on_device(
    history_in,
    history_mid,
    current,
    initial,
    batch_rows,
    halo_rows,
    halo_count,
    adj_cols,
    adj_vals,
    upstream,
    weight_a,
    weight_b,
):
    vmem = pl.BlockSpec(memory_space=pltpu.VMEM)
    smem = pl.BlockSpec(memory_space=pltpu.SMEM)
    hbm = pl.BlockSpec(memory_space=pltpu.HBM)
    sds = jax.ShapeDtypeStruct
    dma = pltpu.SemaphoreType.DMA
    piece = 2 * H // NW
    return pl.pallas_call(
        kernel,
        name="gcn",
        out_shape=(
            sds((BATCH, H), BF16),
            sds((SHARD, H), BF16),
            sds((SHARD, H), BF16),
            sds((H, H), F32),
            sds((H, H), F32),
        ),
        in_specs=[vmem, vmem, vmem, smem] + [hbm] * 8,
        out_specs=(vmem,) * 5,
        scratch_shapes=[
            pltpu.VMEM((NY, CAP, NY * NW), jnp.int32),
            pltpu.VMEM((128, 128), jnp.int32),
            pltpu.VMEM((NW, 1, 128), jnp.int32),
            pltpu.VMEM((NW, 1, 128), jnp.int32),
            pltpu.VMEM((SHARD, 2 * H), BF16),
            pltpu.VMEM((ROWS, SHARD), BF16),
            pltpu.VMEM((NW, NY, 2 * CAP, H), BF16),
            pltpu.VMEM((NY, NW, 2 * CAP, H), BF16),
            pltpu.VMEM((RB + NY, TILE, 2 * H), BF16),
            pltpu.VMEM((RB, NB, TILE, TILE), BF16),
            pltpu.VMEM((NX, BATCH, H), BF16),
            pltpu.VMEM((NX, BATCH, H), BF16),
            pltpu.VMEM((NX, 1, BATCH), jnp.int32),
            pltpu.VMEM((SHARD, NX * BATCH), BF16),
            pltpu.VMEM((SHARD, H), BF16),
            pltpu.VMEM((BATCH, H), BF16),
            pltpu.VMEM((BATCH, H), BF16),
            pltpu.VMEM((H, H), BF16),
            pltpu.VMEM((H, H), BF16),
            pltpu.VMEM((BATCH, 2 * BATCH), BF16),
            pltpu.VMEM((BATCH, 2 * BATCH), BF16),
            pltpu.VMEM((2 * H, H), F32),
            pltpu.VMEM((NW, piece, H), F32),
            pltpu.VMEM((NY, piece, H), F32),
            pltpu.VMEM((NX, piece, H), F32),
            pltpu.VMEM((NW, piece, H), F32),
            dma((8,)),
            dma((2,)),
            dma((2,)),
            dma,
            dma((NY,)),
            dma((6,)),
            dma((8,)),
            pltpu.SemaphoreType.REGULAR,
        ],
        compiler_params=pltpu.CompilerParams(
            collective_id=0, has_side_effects=True, vmem_limit_bytes=40 * 2**20
        ),
    )(
        halo_rows[0].T,
        halo_count,
        batch_rows[None, :],
        adj_cols[0],
        history_in,
        history_mid,
        current,
        initial,
        upstream,
        adj_vals[0],
        weight_a,
        weight_b,
    )


def solution(mesh):
    both = ("node", "rep")
    in_specs = (
        P("node", None),
        P("node", None),
        P(both, None),
        P(both, None),
        P(both),
        P(both, None, None),
        P(both, None),
        P(both, None, None),
        P(both, None, None, None, None),
        P(both, None),
        P(),
        P(),
    )
    out_specs = (P(both, None), P("node", None), P("node", None), P(), P())
    return jax.shard_map(on_device, mesh=mesh, in_specs=in_specs, out_specs=out_specs, check_vma=False)
```

time: 373 us -> 75.1 us (0.20)
  waiting for transfers between devices: 256 us -> 0 us
  Pallas kernels: 0 us -> 62.5 us
  blocking collectives: 58.4 us -> 0 us
  starting transfers between devices: 16.5 us -> 0 us
  between operations: 14.3 us -> 0.69 us
  local copies, waits for them, and re-layouts: 20.4 us -> 11.3 us
  matrix products: 4.32 us -> 0 us
    psum x1 -> x0, waiting for transfers between devices: 251 us -> none  [on_device(): grad_a, grad_b = lax.psum((part_a, part_b), ('node', 'rep'))]
    pallas_call x0 -> x1, Pallas kernels: none -> 62.5 us  [on_device(): pl.pallas_call(kernel, name='gcn', out_shape=(sds((BATCH, H), BF16), sds(...]
    all_to_all x1 -> x0, blocking collectives: 29.7 us -> none  [on_device(): lax.all_to_all(owner_rows, 'node', split_axis=0, concat_axis=0, tiled=True)]
    all_gather x3 -> x0, blocking collectives: 28.7 us -> none  [the longest x1 10.3 us: on_device(): lax.all_gather(current, 'rep', axis=0, tiled=True)]
    all_to_all x2 -> x0, starting transfers between devices: 16.5 us -> none  [the longest x1 10.6 us: on_device(): lax.all_to_all(jnp.take(history_mid, asked_rows, axis=0), 'node', split_a...]
    gather x4 -> x0, local copies, waits for them, and re-layouts: 7.71 us -> none  [the longest x1 3.21 us: on_device(): jnp.take(history_in, asked_rows, axis=0)]
    scatter x2 -> x0, local copies, waits for them, and re-layouts: 6.91 us -> none  [the longest x1 3.46 us: on_device(): history_in_new = history_in.at[all_rows].set(all_current)]
    unnamed x29, local copies, waits for them, and re-layouts: 5.15 us -> 11.3 us
  transfers between devices with their start and end apart: 3 -> 0, of which waited for: 2 -> 0; matrix products, arithmetic and copies ran while one was open for 2% -> 0% of each run, Pallas kernels for 0% -> 0%
where the time goes in v1:
time: 75.1 us; the launch traced here: 74.5 us
  Pallas kernels  62.5 us (83%)
  local copies, waits for them, and re-layouts  11.3 us (15%)
    pallas_call x1, Pallas kernels, on_device(): pl.pallas_call(kernel, name='gcn', out_shape=(sds((BATCH, H), BF16), sds(...  62.5 us
    unnamed x29, local copies, waits for them, and re-layouts  11.3 us

profile of v1, /device:TPU:1, one launch (start us, length us, event | category | flops | bytes accessed | tf_op | source)
XLA Modules:
  0.0 74.5 jit_solution(7443257277010510541)
XLA Ops:
  0.6 0.0 copy-start.8
  0.6 0.0 copy-start.10
  0.7 0.0 copy-start.9
  0.7 0.0 copy-start.11
  0.7 0.6 copy-done.8
  1.3 0.0 copy-done.10
  1.3 0.0 copy-done.9
  1.3 0.0 copy-done.11
  1.4 0.0 copy-start
  1.4 1.0 %copy-done = bf16[2048,128]{1,0:T(8,128)(2,1)S(1)} copy-done((bf16[2048,128]{1,0:T(8,128)(2,1)S(1)}, bf16[2048,128]{1,0:T(8,128)(2,1)}, u32[]{:S(2)}) %copy-start) | copy-done | bytes 524312
  2.4 0.0 copy-start.1
  2.4 1.0 %copy-done.1 = bf16[2048,128]{1,0:T(8,128)(2,1)S(1)} copy-done((bf16[2048,128]{1,0:T(8,128)(2,1)S(1)}, bf16[2048,128]{1,0:T(8,128)(2,1)}, u32[]{:S(2)}) %copy-start.1) | copy-done | bytes 524312
  3.4 1.0 %copy-done.2 = bf16[1,2,8,128,128]{4,3,2,1,0:T(8,128)(2,1)S(1)} copy-done((bf16[1,2,8,128,128]{4,3,2,1,0:T(8,128)(2,1)S(1)}, bf16[1,2,8,128,128]{4,3,2,1,0:T(8,128)(2,1)}, u32[]{:S(2)}) %copy-start.2) | copy-done | bytes 524312
  4.5 0.8 %copy-done.3 = bf16[256,128]{1,0:T(8,128)(2,1)S(1)} copy-done((bf16[256,128]{1,0:T(8,128)(2,1)S(1)}, bf16[256,128]{1,0:T(8,128)(2,1)}, u32[]{:S(2)}) %copy-start.3) | copy-done | bytes 65560
  5.3 0.8 %copy-done.4 = bf16[256,128]{1,0:T(8,128)(2,1)S(1)} copy-done((bf16[256,128]{1,0:T(8,128)(2,1)S(1)}, bf16[256,128]{1,0:T(8,128)(2,1)}, u32[]{:S(2)}) %copy-start.4) | copy-done | bytes 65560
  6.2 0.8 %copy-done.5 = bf16[256,128]{1,0:T(8,128)(2,1)S(1)} copy-done((bf16[256,128]{1,0:T(8,128)(2,1)S(1)}, bf16[256,128]{1,0:T(8,128)(2,1)}, u32[]{:S(2)}) %copy-start.5) | copy-done | bytes 65560
  7.0 0.8 %copy-done.6 = bf16[128,128]{1,0:T(8,128)(2,1)S(1)} copy-done((bf16[128,128]{1,0:T(8,128)(2,1)S(1)}, bf16[128,128]{1,0:T(8,128)(2,1)}, u32[]{:S(2)}) %copy-start.6) | copy-done | bytes 32792
  7.8 0.8 %copy-done.7 = bf16[128,128]{1,0:T(8,128)(2,1)S(1)} copy-done((bf16[128,128]{1,0:T(8,128)(2,1)S(1)}, bf16[128,128]{1,0:T(8,128)(2,1)}, u32[]{:S(2)}) %copy-start.7) | copy-done | bytes 32792
  8.5 62.5 %gcn.1 = (bf16[256,128]{1,0:T(8,128)(2,1)S(1)}, bf16[2048,128]{1,0:T(8,128)(2,1)S(1)}, bf16[2048,128]{1,0:T(8,128)(2,1)S(1)}, f32[128,128]{1,0:T(8,128)S(1)}, f32[128,128]{1,0:T(8,128)S(1)}) custom-call(s32[8,128]{1,0:T(8,128)S(1)} %bitcast.7, s32[1,128]{1,0:T(1,128)S(1)} %copy-done.11, s32[1,256]{1,0:T(1,128)S(1)} %bitcast.8, s32[2,8]{1,0:T(2,128)S(1)} %bitcast.9, ...), custom_call_target="tpu_custom_call" | custom-call | tf_op jit(solution)/shard_map/gcn/pallas_call | solution.py:329
  71.1 0.6 copy.22
  71.7 0.8 %copy.23 = bf16[2048,128]{1,0:T(8,128)(2,1)} copy(bf16[2048,128]{1,0:T(8,128)(2,1)S(1)} %get-tuple-element.11) | data formatting | bytes 1048576
  72.5 0.8 %copy.24 = bf16[2048,128]{1,0:T(8,128)(2,1)} copy(bf16[2048,128]{1,0:T(8,128)(2,1)S(1)} %get-tuple-element.12) | data formatting | bytes 1048576
  73.3 0.6 copy.25
  73.9 0.6 copy.26
  (6 shorter events, 0.0 us)
Async XLA Ops:
  0.6 0.7 copy-start.8
  0.6 0.7 copy-start.10
  0.7 0.7 copy-start.9
  0.7 0.7 copy-start.11
  1.4 1.0 %copy-start = (bf16[2048,128]{1,0:T(8,128)(2,1)S(1)}, bf16[2048,128]{1,0:T(8,128)(2,1)}, u32[]{:S(2)}) copy-start(bf16[2048,128]{1,0:T(8,128)(2,1)} %hist_in.1) | copy-start | bytes 1572868
  2.4 1.0 %copy-start.1 = (bf16[2048,128]{1,0:T(8,128)(2,1)S(1)}, bf16[2048,128]{1,0:T(8,128)(2,1)}, u32[]{:S(2)}) copy-start(bf16[2048,128]{1,0:T(8,128)(2,1)} %hist_mid.1) | copy-start | bytes 1572868
  3.4 1.0 %copy-start.2 = (bf16[1,2,8,128,128]{4,3,2,1,0:T(8,128)(2,1)S(1)}, bf16[1,2,8,128,128]{4,3,2,1,0:T(8,128)(2,1)}, u32[]{:S(2)}) copy-start(bf16[1,2,8,128,128]{4,3,2,1,0:T(8,128)(2,1)} %param.20) | copy-start | bytes 1572868
  4.5 0.8 %copy-start.3 = (bf16[256,128]{1,0:T(8,128)(2,1)S(1)}, bf16[256,128]{1,0:T(8,128)(2,1)}, u32[]{:S(2)}) copy-start(bf16[256,128]{1,0:T(8,128)(2,1)} %current.1) | copy-start | bytes 196612
  5.3 0.8 %copy-start.4 = (bf16[256,128]{1,0:T(8,128)(2,1)S(1)}, bf16[256,128]{1,0:T(8,128)(2,1)}, u32[]{:S(2)}) copy-start(bf16[256,128]{1,0:T(8,128)(2,1)} %initial.1) | copy-start | bytes 196612
  6.2 0.8 %copy-start.5 = (bf16[256,128]{1,0:T(8,128)(2,1)S(1)}, bf16[256,128]{1,0:T(8,128)(2,1)}, u32[]{:S(2)}) copy-start(bf16[256,128]{1,0:T(8,128)(2,1)} %upstream.1) | copy-start | bytes 196612
  7.0 0.8 %copy-start.6 = (bf16[128,128]{1,0:T(8,128)(2,1)S(1)}, bf16[128,128]{1,0:T(8,128)(2,1)}, u32[]{:S(2)}) copy-start(bf16[128,128]{1,0:T(8,128)(2,1)} %weight_a.1) | copy-start | bytes 98308
  7.8 0.8 %copy-start.7 = (bf16[128,128]{1,0:T(8,128)(2,1)S(1)}, bf16[128,128]{1,0:T(8,128)(2,1)}, u32[]{:S(2)}) copy-start(bf16[128,128]{1,0:T(8,128)(2,1)} %weight_b.1) | copy-start | bytes 98308

commit v2 on v1

--- a/solution.py
+++ b/solution.py
@@ -30,6 +30,7 @@
 ROWS = NY * CAP * CHUNK
 PARTS = 8
 BLOCK = SHARD // PARTS
+VMEM = 40 * 2**20
 
 
 def fill(ref, sem):
@@ -48,7 +49,7 @@
     halo_rows,
     halo_count,
     batch_rows,
-    cols,
+    adj_cols,
     hist_in,
     hist_mid,
     current,
@@ -62,6 +63,9 @@
     new_mid,
     grad_a,
     grad_b,
+    list_v,
+    count_v,
+    cols,
     asked_y,
     asked_t,
     ask_row,
@@ -109,6 +113,10 @@
         ).start()
 
     loads = [
+        (halo_rows, list_v),
+        (halo_count, count_v),
+        (batch_rows, br_all.at[x]),
+        (adj_cols, cols),
         (hist_in, hist.at[:, pl.ds(0, H)]),
         (hist_mid, hist.at[:, pl.ds(H, H)]),
         (current, cur_all.at[x]),
@@ -131,8 +139,9 @@
         pl.semaphore_signal(barrier, inc=1, device_id=dev(y, w, (x + k) % NX), device_id_type=MESH)
 
     slot = lax.broadcasted_iota(jnp.int32, (CAP, NY * NW), 0)
-    asked_y[y] = jnp.where(slot < halo_count[...], halo_rows[...], -1)
-    br_all[x] = batch_rows[...]
+    copies[0].wait()
+    copies[1].wait()
+    asked_y[y] = jnp.where(slot < count_v[...], list_v[...], -1)
     pl.semaphore_wait(barrier, NY + NW + NX - 3)
 
     for k in range(1, NY):
@@ -151,6 +160,7 @@
     asked_w[NW - 1] = ask_row[w]
 
     copies[2].wait()
+    copies[6].wait()
     for k in range(1, NX):
         to = dev(y, w, (x + k) % NX)
         send(br_all.at[x], br_all.at[x], rep_sem.at[0], rep_sem.at[1], to)
@@ -167,8 +177,8 @@
             hit = jnp.broadcast_to(wanted[:, i : i + 1], (NY * CAP, SHARD)) == lane
             onehot[pl.ds(q * NY * CAP, NY * CAP), :] = hit.astype(F32).astype(BF16)
         if c == 0:
-            copies[0].wait()
-            copies[1].wait()
+            copies[4].wait()
+            copies[5].wait()
         got = dot(onehot[...], hist[...])
         both = jnp.concatenate(
             [got[:, :H].reshape(CHUNK * NY, CAP, H), got[:, H:].reshape(CHUNK * NY, CAP, H)], 1
@@ -188,6 +198,7 @@
     halo[y, w] = rows_out[NW - 1, y]
 
     copies[3].wait()
+    copies[7].wait()
     for r in range(RB):
         for c in range(RB):
             acc = jnp.zeros((TILE, TILE), F32)
@@ -220,7 +231,7 @@
         kept = put[:, H:] == 0.0
         new_in[rows, :] = jnp.where(kept, hist[rows, pl.ds(0, H)].astype(F32), put[:, :H]).astype(BF16)
         base_mid[rows, :] = jnp.where(kept, hist[rows, pl.ds(H, H)].astype(F32), 0.0).astype(BF16)
-    for c in copies[4:]:
+    for c in copies[8:]:
         c.wait()
 
     for k in range(NY):
@@ -306,6 +317,15 @@
     fill(total.at[pl.ds(0, NW - 1)], red_sem.at[6])
 
 
+def write_out(*refs):
+    sems = refs[-1]
+    copies = [pltpu.make_async_copy(refs[i], refs[5 + i], sems.at[i]) for i in range(5)]
+    for c in copies:
+        c.start()
+    for c in copies:
+        c.wait()
+
+
 def on_device(
     history_in,
     history_mid,
@@ -321,12 +341,11 @@
     weight_b,
 ):
     vmem = pl.BlockSpec(memory_space=pltpu.VMEM)
-    smem = pl.BlockSpec(memory_space=pltpu.SMEM)
     hbm = pl.BlockSpec(memory_space=pltpu.HBM)
     sds = jax.ShapeDtypeStruct
     dma = pltpu.SemaphoreType.DMA
     piece = 2 * H // NW
-    return pl.pallas_call(
+    results = pl.pallas_call(
         kernel,
         name="gcn",
         out_shape=(
@@ -336,9 +355,12 @@
             sds((H, H), F32),
             sds((H, H), F32),
         ),
-        in_specs=[vmem, vmem, vmem, smem] + [hbm] * 8,
+        in_specs=[hbm] * 12,
         out_specs=(vmem,) * 5,
         scratch_shapes=[
+            pltpu.VMEM((CAP, NY * NW), jnp.int32),
+            pltpu.VMEM((1, NY * NW), jnp.int32),
+            pltpu.SMEM((RB, NB), jnp.int32),
             pltpu.VMEM((NY, CAP, NY * NW), jnp.int32),
             pltpu.VMEM((128, 128), jnp.int32),
             pltpu.VMEM((NW, 1, 128), jnp.int32),
@@ -365,7 +387,7 @@
             pltpu.VMEM((NY, piece, H), F32),
             pltpu.VMEM((NX, piece, H), F32),
             pltpu.VMEM((NW, piece, H), F32),
-            dma((8,)),
+            dma((12,)),
             dma((2,)),
             dma((2,)),
             dma,
@@ -375,9 +397,9 @@
             pltpu.SemaphoreType.REGULAR,
         ],
         compiler_params=pltpu.CompilerParams(
-            collective_id=0, has_side_effects=True, vmem_limit_bytes=40 * 2**20
+            collective_id=0, has_side_effects=True, vmem_limit_bytes=VMEM
         ),
-    )(
+    )(*[pltpu.with_memory_space_constraint(a, pltpu.HBM) for a in (
         halo_rows[0].T,
         halo_count,
         batch_rows[None, :],
@@ -390,7 +412,16 @@
         adj_vals[0],
         weight_a,
         weight_b,
-    )
+    )])
+    return pl.pallas_call(
+        write_out,
+        name="write_out",
+        out_shape=tuple(sds(r.shape, r.dtype) for r in results),
+        in_specs=[vmem] * 5,
+        out_specs=(hbm,) * 5,
+        scratch_shapes=[dma((5,))],
+        compiler_params=pltpu.CompilerParams(vmem_limit_bytes=4 * 2**20),
+    )(*results)
 
 
 def solution(mesh):

time: 75.1 us -> 63.7 us (0.85)
  local copies, waits for them, and re-layouts: 11.3 us -> 0 us
    unnamed x29 -> x0, local copies, waits for them, and re-layouts: 11.3 us -> none
    pallas_call x0 -> x1, Pallas kernels: none -> 1.06 us  [on_device(): pl.pallas_call(write_out, name='write_out', out_shape=tuple((sds(r.shape,...]
where the time goes in v2:
time: 63.7 us; the launch traced here: 63.6 us
  Pallas kernels  63 us (99%)
  between operations  0.64 us (1%)
    pallas_call x1, Pallas kernels, on_device(): pl.pallas_call(kernel, name='gcn', out_shape=(sds((BATCH, H), BF16), sds(...  61.9 us

profile of v2, /device:TPU:1, one launch (start us, length us, event | category | flops | bytes accessed | tf_op | source)
XLA Modules:
  0.0 63.6 jit_solution(7681191186426191593)
XLA Ops:
  0.6 61.9 %gcn.1 = (bf16[256,128]{1,0:T(8,128)(2,1)S(1)}, bf16[2048,128]{1,0:T(8,128)(2,1)S(1)}, bf16[2048,128]{1,0:T(8,128)(2,1)S(1)}, f32[128,128]{1,0:T(8,128)S(1)}, f32[128,128]{1,0:T(8,128)S(1)}) custom-call(s32[8,128]{1,0:T(8,128)} %bitcast.7, s32[1,128]{1,0:T(1,128)} %halo_count.1, s32[1,256]{1,0:T(1,128)} %bitcast.8, s32[2,8]{1,0:T(2,128)} %bitcast.9, ...), custom_call_target="tpu_custom_call" | custom-call | tf_op jit(solution)/shard_map/gcn/pallas_call | solution.py:348
  62.5 1.1 %write_out.1 = (bf16[256,128]{1,0:T(8,128)(2,1)}, bf16[2048,128]{1,0:T(8,128)(2,1)}, bf16[2048,128]{1,0:T(8,128)(2,1)}, f32[128,128]{1,0:T(8,128)}, f32[128,128]{1,0:T(8,128)}) custom-call(bf16[256,128]{1,0:T(8,128)(2,1)S(1)} %get-tuple-element.10.refs_0_, bf16[2048,128]{1,0:T(8,128)(2,1)S(1)} %get-tuple-element.11.refs_1_, ...), custom_call_target="tpu_custom_call" | custom-call | tf_op jit(solution)/shard_map/write_out/pallas_call | solution.py:416

commit v3 on v2

--- a/solution.py
+++ b/solution.py
@@ -25,9 +25,34 @@
 SHARD = 2048
 RB = 2
 NB = 8
-W_ORDER = (8, 7, 9, 6, 10, 5, 11, 4, 12, 3, 13, 2, 14, 1, 15, 0)
+NZ = 8
+CORES = 2
+FAR = (4, 3, 5, 2, 6, 1, 7, 0)
+W_ORDER = (8, 7, 9, 6, 10, 5, 11, 4, 12, 3, 13, 2, 14, 1, 15)
+X_ORDER = (2, 1, 3)
 CHUNK = 4
 ROWS = NY * CAP * CHUNK
+WAVES = 4
+
+
+def hops(pair):
+    j, ky = pair
+    dz, dy = min(FAR[j], NZ - FAR[j]), min(ky, NY - ky)
+    return -max(dz, dy), -dz - dy
+
+
+def schedule():
+    steps, left = [], []
+    for c, some in enumerate((8, 6, 6, 64)):
+        left = sorted(left + [(j, ky) for j in (2 * c, 2 * c + 1) for ky in FAR], key=hops)
+        steps.append(left[:some])
+        left = left[some:]
+    return steps
+
+
+STEPS = schedule()
+ORDER = [pair for step in STEPS for pair in step]
+WAVE = {pair: i * WAVES // len(ORDER) for i, pair in enumerate(ORDER)}
 PARTS = 8
 BLOCK = SHARD // PARTS
 VMEM = 40 * 2**20
@@ -103,6 +128,7 @@
 ):
     node, x = lax.axis_index("node"), lax.axis_index("rep")
     y, w = node // NW, node % NW
+    z, core = w // CORES, w % CORES
 
     def dev(yy, ww, xx):
         return (yy * NW + ww, xx)
@@ -131,9 +157,9 @@
         c.start()
 
     barrier = pltpu.get_barrier_semaphore()
-    for k in range(1, NY):
+    for k in FAR[:-1]:
         pl.semaphore_signal(barrier, inc=1, device_id=dev((y + k) % NY, w, x), device_id_type=MESH)
-    for k in range(1, NW):
+    for k in W_ORDER:
         pl.semaphore_signal(barrier, inc=1, device_id=dev(y, (w + k) % NW, x), device_id_type=MESH)
     for k in range(1, NX):
         pl.semaphore_signal(barrier, inc=1, device_id=dev(y, w, (x + k) % NX), device_id_type=MESH)
@@ -144,7 +170,7 @@
     asked_y[y] = jnp.where(slot < count_v[...], list_v[...], -1)
     pl.semaphore_wait(barrier, NY + NW + NX - 3)
 
-    for k in range(1, NY):
+    for k in FAR[:-1]:
         send(asked_y.at[y], asked_y.at[y], y_sem.at[0], y_sem.at[1], dev((y + k) % NY, w, x))
     fill(asked_y.at[pl.ds(0, NY - 1)], y_sem.at[1])
     lists = asked_y[...].reshape(NY * CAP, NY * NW)
@@ -153,15 +179,16 @@
     mine = asked_t[pl.ds(pl.multiple_of(y * NW, NW), NW), :]
     for i in range(NW):
         ask_row[i] = mine[i : i + 1, :]
-    for i, k in enumerate(W_ORDER):
-        if k:
-            to = (w + k) % NW
-            send(ask_row.at[to], asked_w.at[i], w_sem.at[0], w_sem.at[1], dev(y, to, x))
-    asked_w[NW - 1] = ask_row[w]
+    for j, k in enumerate(FAR):
+        for other in range(CORES):
+            if k or other:
+                to = (z + NZ - k) % NZ * CORES + (core + other) % CORES
+                send(ask_row.at[to], asked_w.at[CORES * j + core], w_sem.at[0], w_sem.at[1], dev(y, to, x))
+    asked_w[NW - CORES + core] = ask_row[w]
 
     copies[2].wait()
     copies[6].wait()
-    for k in range(1, NX):
+    for k in X_ORDER:
         to = dev(y, w, (x + k) % NX)
         send(br_all.at[x], br_all.at[x], rep_sem.at[0], rep_sem.at[1], to)
         send(cur_all.at[x], cur_all.at[x], rep_sem.at[2], rep_sem.at[3], to)
@@ -184,18 +211,15 @@
             [got[:, :H].reshape(CHUNK * NY, CAP, H), got[:, H:].reshape(CHUNK * NY, CAP, H)], 1
         )
         rows_out[pl.ds(c * CHUNK, CHUNK)] = both.astype(BF16).reshape(CHUNK, NY, 2 * CAP, H)
-        for q in range(CHUNK):
-            i = c * CHUNK + q
-            k = W_ORDER[i]
-            to_w = (w + NW - k) % NW
-
-            def reply(ky, carry, i=i, to_w=to_w):
-                to_y = (y + ky) % NY
-                send(rows_out.at[i, to_y], halo.at[y, w], h_send, h_recv.at[y], dev(to_y, to_w, x))
-                return carry
-
-            lax.fori_loop(0 if k else 1, NY, reply, 0)
-    halo[y, w] = rows_out[NW - 1, y]
+        for j, ky in STEPS[c]:
+            for other in range(CORES):
+                if FAR[j] or ky or other:
+                    to_core, to_y = (core + other) % CORES, (y + ky) % NY
+                    to_w = (z + FAR[j]) % NZ * CORES + to_core
+                    src = rows_out.at[CORES * j + to_core, to_y]
+                    dst = halo.at[(j * NY + y) * CORES + core]
+                    send(src, dst, h_send, h_recv.at[WAVE[j, ky]], dev(to_y, to_w, x))
+    halo[((NZ - 1) * NY + y) * CORES + core] = rows_out[NW - CORES + core, y]
 
     copies[3].wait()
     copies[7].wait()
@@ -234,16 +258,16 @@
     for c in copies[8:]:
         c.wait()
 
-    for k in range(NY):
-        yy = (y + k) % NY
-        if k:
-            fill(halo.at[yy], h_recv.at[yy])
-        else:
-            fill(halo.at[y, pl.ds(0, NW - 1)], h_recv.at[y])
-        block = halo[yy].astype(F32)
-        pair = [block[:, :CAP, :].reshape(TILE, H), block[:, CAP:, :].reshape(TILE, H)]
-        tiles[RB + yy] = jnp.concatenate(pair, 1).astype(BF16)
-    for k in range(1, NX):
+    for wave in range(WAVES):
+        pairs = [pair for pair in ORDER if WAVE[pair] == wave]
+        fill(halo.at[pl.ds(0, len(pairs) * CORES - (1 if (NZ - 1, 0) in pairs else 0))], h_recv.at[wave])
+        for j, ky in pairs:
+            yy, zz = (y + NY - ky) % NY, (z + NZ - FAR[j]) % NZ
+            block = halo[pl.ds((j * NY + yy) * CORES, CORES)].astype(F32)
+            both = [block[:, :CAP, :].reshape(CORES * CAP, H), block[:, CAP:, :].reshape(CORES * CAP, H)]
+            rows = pl.ds(pl.multiple_of(zz * CORES * CAP, CORES * CAP), CORES * CAP)
+            tiles[RB + yy, rows, :] = jnp.concatenate(both, 1).astype(BF16)
+    for k in X_ORDER:
         pl.semaphore_signal(ready, inc=1, device_id=dev(y, w, (x + k) % NX), device_id_type=MESH)
 
     sums = []
@@ -257,38 +281,38 @@
     preact_a = (1.0 - BETA_A) * support_a.astype(F32) + BETA_A * dot(support_a, wa_v[...])
     fresh = jnp.maximum(preact_a, 0.0).astype(BF16)
     fresh_all[x] = fresh
-    for k in range(1, NX):
+    for k in X_ORDER:
         send(fresh_all.at[x], fresh_all.at[x], rep_sem.at[4], rep_sem.at[5], dev(y, w, (x + k) % NX))
     agg_b = agg[:, H:] + dot(f_fwd[...], jnp.concatenate([fresh, fresh], 0))
     support_b = ((1.0 - ALPHA) * agg_b + init).astype(BF16)
     preact_b = (1.0 - BETA_B) * support_b.astype(F32) + BETA_B * dot(support_b, wb_v[...])
     final_out[...] = jnp.maximum(preact_b, 0.0).astype(BF16)
     gated_b = jnp.where(preact_b > 0, up_v[...].astype(F32), 0.0).astype(BF16)
-    part[pl.ds(H, H), :] = BETA_B * dot_t(support_b, gated_b)
+    part[pl.ds(H, H), :] = (BETA_B * dot_t(support_b, gated_b)).astype(BF16)
     back = lax.dot_general(gated_b, wb_v[...], (((1,), (1,)), ((), ())), preferred_element_type=F32)
     support_grad = (1.0 - BETA_B) * gated_b.astype(F32) + BETA_B * back
     agg_grad = ((1.0 - ALPHA) * support_grad).astype(BF16)
     fresh_grad = dot(f_bwd[...], jnp.concatenate([agg_grad, agg_grad], 0))
     gated_a = jnp.where(preact_a > 0, fresh_grad, 0.0).astype(BF16)
-    part[pl.ds(0, H), :] = BETA_A * dot_t(support_a, gated_a)
+    part[pl.ds(0, H), :] = (BETA_A * dot_t(support_a, gated_a)).astype(BF16)
 
     piece = 2 * H // NW
-    for k in W_ORDER[:-1]:
+    for k in W_ORDER:
         to = (w + k) % NW
         rows = pl.ds(pl.multiple_of(to * piece, piece), piece)
         send(part.at[rows, :], sum_w.at[w], red_sem.at[0], red_sem.at[1], dev(y, to, x))
     sum_w[w] = part[pl.ds(pl.multiple_of(w * piece, piece), piece), :]
     fill(sum_w.at[pl.ds(0, NW - 1)], red_sem.at[1])
-    sum_y[y] = jnp.sum(sum_w[...], 0)
-    for k in range(1, NY):
+    sum_y[y] = jnp.sum(sum_w[...].astype(F32), 0)
+    for k in FAR[:-1]:
         send(sum_y.at[y], sum_y.at[y], red_sem.at[2], red_sem.at[3], dev((y + k) % NY, w, x))
     fill(sum_y.at[pl.ds(0, NY - 1)], red_sem.at[3])
     sum_x[x] = jnp.sum(sum_y[...], 0)
-    for k in range(1, NX):
+    for k in X_ORDER:
         send(sum_x.at[x], sum_x.at[x], red_sem.at[4], red_sem.at[5], dev(y, w, (x + k) % NX))
     fill(sum_x.at[pl.ds(0, NX - 1)], red_sem.at[5])
-    total[w] = jnp.sum(sum_x[...], 0) * (1.0 / math.sqrt(NY * NW * NX * BATCH))
-    for k in W_ORDER[:-1]:
+    total[w] = (jnp.sum(sum_x[...], 0) * (1.0 / math.sqrt(NY * NW * NX * BATCH))).astype(BF16)
+    for k in W_ORDER:
         send(total.at[w], total.at[w], red_sem.at[6], red_sem.at[7], dev(y, (w + k) % NW, x))
 
     pl.semaphore_wait(ready, NX - 1)
@@ -301,16 +325,15 @@
 
     fill(total.at[pl.ds(0, NW - 1)], red_sem.at[7])
     half = NW // 2
-    grad_a[...] = total[pl.ds(0, half)].reshape(H, H)
-    grad_b[...] = total[pl.ds(half, half)].reshape(H, H)
+    grad_a[...] = total[pl.ds(0, half)].astype(F32).reshape(H, H)
+    grad_b[...] = total[pl.ds(half, half)].astype(F32).reshape(H, H)
 
     fill(asked_y.at[pl.ds(0, NY - 1)], y_sem.at[0])
     fill(asked_w.at[pl.ds(0, NW - 1)], w_sem.at[0])
     fill(br_all.at[pl.ds(0, NX - 1)], rep_sem.at[0])
     fill(cur_all.at[pl.ds(0, NX - 1)], rep_sem.at[2])
     fill(fresh_all.at[pl.ds(0, NX - 1)], rep_sem.at[4])
-    for k in range(NY):
-        fill(halo.at[k] if k else halo.at[k, pl.ds(0, NW - 1)], h_send)
+    fill(halo.at[pl.ds(0, NY * NW - 1)], h_send)
     fill(sum_w.at[pl.ds(0, NW - 1)], red_sem.at[0])
     fill(sum_y.at[pl.ds(0, NY - 1)], red_sem.at[2])
     fill(sum_x.at[pl.ds(0, NX - 1)], red_sem.at[4])
@@ -368,7 +391,7 @@
             pltpu.VMEM((SHARD, 2 * H), BF16),
             pltpu.VMEM((ROWS, SHARD), BF16),
             pltpu.VMEM((NW, NY, 2 * CAP, H), BF16),
-            pltpu.VMEM((NY, NW, 2 * CAP, H), BF16),
+            pltpu.VMEM((NY * NW, 2 * CAP, H), BF16),
             pltpu.VMEM((RB + NY, TILE, 2 * H), BF16),
             pltpu.VMEM((RB, NB, TILE, TILE), BF16),
             pltpu.VMEM((NX, BATCH, H), BF16),
@@ -382,16 +405,16 @@
             pltpu.VMEM((H, H), BF16),
             pltpu.VMEM((BATCH, 2 * BATCH), BF16),
             pltpu.VMEM((BATCH, 2 * BATCH), BF16),
-            pltpu.VMEM((2 * H, H), F32),
-            pltpu.VMEM((NW, piece, H), F32),
+            pltpu.VMEM((2 * H, H), BF16),
+            pltpu.VMEM((NW, piece, H), BF16),
             pltpu.VMEM((NY, piece, H), F32),
             pltpu.VMEM((NX, piece, H), F32),
-            pltpu.VMEM((NW, piece, H), F32),
+            pltpu.VMEM((NW, piece, H), BF16),
             dma((12,)),
             dma((2,)),
             dma((2,)),
             dma,
-            dma((NY,)),
+            dma((WAVES,)),
             dma((6,)),
             dma((8,)),
             pltpu.SemaphoreType.REGULAR,

time: 63.7 us -> 61.6 us (0.967)
  Pallas kernels: 63 us -> 60.8 us
    pallas_call x1, Pallas kernels: 61.9 us -> 59.8 us  [on_device(): pl.pallas_call(kernel, name='gcn', out_shape=(sds((BATCH, H), BF16), sds(...]
where the time goes in v3:
time: 61.6 us; the launch traced here: 61.5 us
  Pallas kernels  60.8 us (99%)
  between operations  0.64 us (1%)
    pallas_call x1, Pallas kernels, on_device(): pl.pallas_call(kernel, name='gcn', out_shape=(sds((BATCH, H), BF16), sds(...  59.8 us

profile of v3, /device:TPU:1, one launch (start us, length us, event | category | flops | bytes accessed | tf_op | source)
XLA Modules:
  0.0 61.5 jit_solution(9223341868846120829)
XLA Ops:
  0.6 59.8 %gcn.1 = (bf16[256,128]{1,0:T(8,128)(2,1)S(1)}, bf16[2048,128]{1,0:T(8,128)(2,1)S(1)}, bf16[2048,128]{1,0:T(8,128)(2,1)S(1)}, f32[128,128]{1,0:T(8,128)S(1)}, f32[128,128]{1,0:T(8,128)S(1)}) custom-call(s32[8,128]{1,0:T(8,128)} %bitcast.7, s32[1,128]{1,0:T(1,128)} %halo_count.1, s32[1,256]{1,0:T(1,128)} %bitcast.8, s32[2,8]{1,0:T(2,128)} %bitcast.9, ...), custom_call_target="tpu_custom_call" | custom-call | tf_op jit(solution)/shard_map/gcn/pallas_call | solution.py:371
  60.4 1.1 %write_out.1 = (bf16[256,128]{1,0:T(8,128)(2,1)}, bf16[2048,128]{1,0:T(8,128)(2,1)}, bf16[2048,128]{1,0:T(8,128)(2,1)}, f32[128,128]{1,0:T(8,128)}, f32[128,128]{1,0:T(8,128)}) custom-call(bf16[256,128]{1,0:T(8,128)(2,1)S(1)} %get-tuple-element.10.refs_0_, bf16[2048,128]{1,0:T(8,128)(2,1)S(1)} %get-tuple-element.11.refs_1_, ...), custom_call_target="tpu_custom_call" | custom-call | tf_op jit(solution)/shard_map/write_out/pallas_call | solution.py:439

commit v4 on v3

--- a/solution.py
+++ b/solution.py
@@ -1,4 +1,3 @@
-import functools
 import math
 
 import jax
@@ -33,6 +32,9 @@
 CHUNK = 4
 ROWS = NY * CAP * CHUNK
 WAVES = 4
+GROUP = NX * CORES
+PIECE = 2 * H // GROUP
+SCALE = 1.0 / math.sqrt(NY * NW * NX * BATCH)
 
 
 def hops(pair):
@@ -113,9 +115,9 @@
     f_fwd,
     f_bwd,
     part,
-    sum_w,
+    sum_g,
+    sum_z,
     sum_y,
-    sum_x,
     total,
     load_sem,
     y_sem,
@@ -124,7 +126,6 @@
     h_recv,
     rep_sem,
     red_sem,
-    ready,
 ):
     node, x = lax.axis_index("node"), lax.axis_index("rep")
     y, w = node // NW, node % NW
@@ -267,8 +268,6 @@
             both = [block[:, :CAP, :].reshape(CORES * CAP, H), block[:, CAP:, :].reshape(CORES * CAP, H)]
             rows = pl.ds(pl.multiple_of(zz * CORES * CAP, CORES * CAP), CORES * CAP)
             tiles[RB + yy, rows, :] = jnp.concatenate(both, 1).astype(BF16)
-    for k in X_ORDER:
-        pl.semaphore_signal(ready, inc=1, device_id=dev(y, w, (x + k) % NX), device_id_type=MESH)
 
     sums = []
     for r in range(RB):
@@ -281,8 +280,6 @@
     preact_a = (1.0 - BETA_A) * support_a.astype(F32) + BETA_A * dot(support_a, wa_v[...])
     fresh = jnp.maximum(preact_a, 0.0).astype(BF16)
     fresh_all[x] = fresh
-    for k in X_ORDER:
-        send(fresh_all.at[x], fresh_all.at[x], rep_sem.at[4], rep_sem.at[5], dev(y, w, (x + k) % NX))
     agg_b = agg[:, H:] + dot(f_fwd[...], jnp.concatenate([fresh, fresh], 0))
     support_b = ((1.0 - ALPHA) * agg_b + init).astype(BF16)
     preact_b = (1.0 - BETA_B) * support_b.astype(F32) + BETA_B * dot(support_b, wb_v[...])
@@ -296,26 +293,33 @@
     gated_a = jnp.where(preact_a > 0, fresh_grad, 0.0).astype(BF16)
     part[pl.ds(0, H), :] = (BETA_A * dot_t(support_a, gated_a)).astype(BF16)
 
-    piece = 2 * H // NW
-    for k in W_ORDER:
-        to = (w + k) % NW
-        rows = pl.ds(pl.multiple_of(to * piece, piece), piece)
-        send(part.at[rows, :], sum_w.at[w], red_sem.at[0], red_sem.at[1], dev(y, to, x))
-    sum_w[w] = part[pl.ds(pl.multiple_of(w * piece, piece), piece), :]
-    fill(sum_w.at[pl.ds(0, NW - 1)], red_sem.at[1])
-    sum_y[y] = jnp.sum(sum_w[...].astype(F32), 0)
+    group = x * CORES + core
+    friends = []
+    for k in X_ORDER + (0,):
+        for other in range(CORES):
+            if k or other:
+                to_x, to_core = (x + k) % NX, (core + other) % CORES
+                friends.append((to_x * CORES + to_core, dev(y, z * CORES + to_core, to_x)))
+    for to, device in friends:
+        rows = pl.ds(pl.multiple_of(to * PIECE, PIECE), PIECE)
+        send(part.at[rows, :], sum_g.at[group], red_sem.at[0], red_sem.at[1], device)
+    sum_g[group] = part[pl.ds(pl.multiple_of(group * PIECE, PIECE), PIECE), :]
+    fill(sum_g.at[pl.ds(0, GROUP - 1)], red_sem.at[1])
+    sum_z[z] = jnp.sum(sum_g[...].astype(F32), 0).astype(BF16)
     for k in FAR[:-1]:
-        send(sum_y.at[y], sum_y.at[y], red_sem.at[2], red_sem.at[3], dev((y + k) % NY, w, x))
-    fill(sum_y.at[pl.ds(0, NY - 1)], red_sem.at[3])
-    sum_x[x] = jnp.sum(sum_y[...], 0)
+        to = (z + k) % NZ * CORES + core
+        send(sum_z.at[z], sum_z.at[z], red_sem.at[2], red_sem.at[3], dev(y, to, x))
     for k in X_ORDER:
-        send(sum_x.at[x], sum_x.at[x], red_sem.at[4], red_sem.at[5], dev(y, w, (x + k) % NX))
-    fill(sum_x.at[pl.ds(0, NX - 1)], red_sem.at[5])
-    total[w] = (jnp.sum(sum_x[...], 0) * (1.0 / math.sqrt(NY * NW * NX * BATCH))).astype(BF16)
-    for k in W_ORDER:
-        send(total.at[w], total.at[w], red_sem.at[6], red_sem.at[7], dev(y, (w + k) % NW, x))
-
-    pl.semaphore_wait(ready, NX - 1)
+        send(fresh_all.at[x], fresh_all.at[x], rep_sem.at[4], rep_sem.at[5], dev(y, w, (x + k) % NX))
+    fill(sum_z.at[pl.ds(0, NZ - 1)], red_sem.at[3])
+    sum_y[y] = jnp.sum(sum_z[...].astype(F32), 0).astype(BF16)
+    for k in FAR[:-1]:
+        send(sum_y.at[y], sum_y.at[y], red_sem.at[4], red_sem.at[5], dev((y + k) % NY, w, x))
+    fill(sum_y.at[pl.ds(0, NY - 1)], red_sem.at[5])
+    total[group] = (jnp.sum(sum_y[...].astype(F32), 0) * SCALE).astype(BF16)
+    for _, device in friends:
+        send(total.at[group], total.at[group], red_sem.at[6], red_sem.at[7], device)
+
     fill(fresh_all.at[pl.ds(0, NX - 1)], rep_sem.at[5])
     fresh_rows = fresh_all[...].reshape(NX * BATCH, H)
     for p in range(PARTS):
@@ -323,8 +327,8 @@
         put = dot(refresh[rows, :], fresh_rows)
         new_mid[rows, :] = (put + base_mid[rows, :].astype(F32)).astype(BF16)
 
-    fill(total.at[pl.ds(0, NW - 1)], red_sem.at[7])
-    half = NW // 2
+    fill(total.at[pl.ds(0, GROUP - 1)], red_sem.at[7])
+    half = GROUP // 2
     grad_a[...] = total[pl.ds(0, half)].astype(F32).reshape(H, H)
     grad_b[...] = total[pl.ds(half, half)].astype(F32).reshape(H, H)
 
@@ -334,10 +338,10 @@
     fill(cur_all.at[pl.ds(0, NX - 1)], rep_sem.at[2])
     fill(fresh_all.at[pl.ds(0, NX - 1)], rep_sem.at[4])
     fill(halo.at[pl.ds(0, NY * NW - 1)], h_send)
-    fill(sum_w.at[pl.ds(0, NW - 1)], red_sem.at[0])
-    fill(sum_y.at[pl.ds(0, NY - 1)], red_sem.at[2])
-    fill(sum_x.at[pl.ds(0, NX - 1)], red_sem.at[4])
-    fill(total.at[pl.ds(0, NW - 1)], red_sem.at[6])
+    fill(sum_g.at[pl.ds(0, GROUP - 1)], red_sem.at[0])
+    fill(sum_z.at[pl.ds(0, NZ - 1)], red_sem.at[2])
+    fill(sum_y.at[pl.ds(0, NY - 1)], red_sem.at[4])
+    fill(total.at[pl.ds(0, GROUP - 1)], red_sem.at[6])
 
 
 def write_out(*refs):
@@ -367,7 +371,6 @@
     hbm = pl.BlockSpec(memory_space=pltpu.HBM)
     sds = jax.ShapeDtypeStruct
     dma = pltpu.SemaphoreType.DMA
-    piece = 2 * H // NW
     results = pl.pallas_call(
         kernel,
         name="gcn",
@@ -406,10 +409,10 @@
             pltpu.VMEM((BATCH, 2 * BATCH), BF16),
             pltpu.VMEM((BATCH, 2 * BATCH), BF16),
             pltpu.VMEM((2 * H, H), BF16),
-            pltpu.VMEM((NW, piece, H), BF16),
-            pltpu.VMEM((NY, piece, H), F32),
-            pltpu.VMEM((NX, piece, H), F32),
-            pltpu.VMEM((NW, piece, H), BF16),
+            pltpu.VMEM((GROUP, PIECE, H), BF16),
+            pltpu.VMEM((NZ, PIECE, H), BF16),
+            pltpu.VMEM((NY, PIECE, H), BF16),
+            pltpu.VMEM((GROUP, PIECE, H), BF16),
             dma((12,)),
             dma((2,)),
             dma((2,)),
@@ -417,7 +420,6 @@
             dma((WAVES,)),
             dma((6,)),
             dma((8,)),
-            pltpu.SemaphoreType.REGULAR,
         ],
         compiler_params=pltpu.CompilerParams(
             collective_id=0, has_side_effects=True, vmem_limit_bytes=VMEM

time: 61.6 us -> 60.1 us (0.976)
  Pallas kernels: 60.8 us -> 59.3 us
    pallas_call x1, Pallas kernels: 59.8 us -> 58.2 us  [on_device(): pl.pallas_call(kernel, name='gcn', out_shape=(sds((BATCH, H), BF16), sds(...]
where the time goes in v4:
time: 60.1 us; the launch traced here: 60 us
  Pallas kernels  59.3 us (99%)
  between operations  0.64 us (1%)
    pallas_call x1, Pallas kernels, on_device(): pl.pallas_call(kernel, name='gcn', out_shape=(sds((BATCH, H), BF16), sds(...  58.2 us

profile of v4, /device:TPU:1, one launch (start us, length us, event | category | flops | bytes accessed | tf_op | source)
XLA Modules:
  0.0 60.0 jit_solution(15071262855433510524)
XLA Ops:
  0.6 58.2 %gcn.1 = (bf16[256,128]{1,0:T(8,128)(2,1)S(1)}, bf16[2048,128]{1,0:T(8,128)(2,1)S(1)}, bf16[2048,128]{1,0:T(8,128)(2,1)S(1)}, f32[128,128]{1,0:T(8,128)S(1)}, f32[128,128]{1,0:T(8,128)S(1)}) custom-call(s32[8,128]{1,0:T(8,128)} %bitcast.7, s32[1,128]{1,0:T(1,128)} %halo_count.1, s32[1,256]{1,0:T(1,128)} %bitcast.8, s32[2,8]{1,0:T(2,128)} %bitcast.9, ...), custom_call_target="tpu_custom_call" | custom-call | tf_op jit(solution)/shard_map/gcn/pallas_call | solution.py:374
  58.9 1.1 %write_out.1 = (bf16[256,128]{1,0:T(8,128)(2,1)}, bf16[2048,128]{1,0:T(8,128)(2,1)}, bf16[2048,128]{1,0:T(8,128)(2,1)}, f32[128,128]{1,0:T(8,128)}, f32[128,128]{1,0:T(8,128)}) custom-call(bf16[256,128]{1,0:T(8,128)(2,1)S(1)} %get-tuple-element.10.refs_0_, bf16[2048,128]{1,0:T(8,128)(2,1)S(1)} %get-tuple-element.11.refs_1_, ...), custom_call_target="tpu_custom_call" | custom-call | tf_op jit(solution)/shard_map/write_out/pallas_call | solution.py:441

commit v5 on v4

--- a/solution.py
+++ b/solution.py
@@ -29,8 +29,8 @@
 FAR = (4, 3, 5, 2, 6, 1, 7, 0)
 W_ORDER = (8, 7, 9, 6, 10, 5, 11, 4, 12, 3, 13, 2, 14, 1, 15)
 X_ORDER = (2, 1, 3)
-CHUNK = 4
-ROWS = NY * CAP * CHUNK
+CHUNKS = ((0,), (1,), (2, 3), (4, 5), (6, 7))
+ROWS = NY * CAP * CORES * 2
 WAVES = 4
 GROUP = NX * CORES
 PIECE = 2 * H // GROUP
@@ -45,8 +45,8 @@
 
 def schedule():
     steps, left = [], []
-    for c, some in enumerate((8, 6, 6, 64)):
-        left = sorted(left + [(j, ky) for j in (2 * c, 2 * c + 1) for ky in FAR], key=hops)
+    for chunk, some in zip(CHUNKS, (8, 4, 6, 6, 64)):
+        left = sorted(left + [(j, ky) for j in chunk for ky in FAR], key=hops)
         steps.append(left[:some])
         left = left[some:]
     return steps
@@ -154,8 +154,8 @@
         (weight_b, wb_v),
     ]
     copies = [pltpu.make_async_copy(s, d, load_sem.at[i]) for i, (s, d) in enumerate(loads)]
-    for c in copies:
-        c.start()
+    copies[0].start()
+    copies[1].start()
 
     barrier = pltpu.get_barrier_semaphore()
     for k in FAR[:-1]:
@@ -173,6 +173,15 @@
 
     for k in FAR[:-1]:
         send(asked_y.at[y], asked_y.at[y], y_sem.at[0], y_sem.at[1], dev((y + k) % NY, w, x))
+    for c in copies[2:]:
+        c.start()
+    copies[2].wait()
+    copies[6].wait()
+    for k in X_ORDER:
+        to = dev(y, w, (x + k) % NX)
+        send(br_all.at[x], br_all.at[x], rep_sem.at[0], rep_sem.at[1], to)
+        send(cur_all.at[x], cur_all.at[x], rep_sem.at[2], rep_sem.at[3], to)
+
     fill(asked_y.at[pl.ds(0, NY - 1)], y_sem.at[1])
     lists = asked_y[...].reshape(NY * CAP, NY * NW)
     lists = jnp.concatenate([lists, jnp.zeros((128 - NY * CAP, NY * NW), jnp.int32)], 0)
@@ -187,31 +196,22 @@
                 send(ask_row.at[to], asked_w.at[CORES * j + core], w_sem.at[0], w_sem.at[1], dev(y, to, x))
     asked_w[NW - CORES + core] = ask_row[w]
 
-    copies[2].wait()
-    copies[6].wait()
-    for k in X_ORDER:
-        to = dev(y, w, (x + k) % NX)
-        send(br_all.at[x], br_all.at[x], rep_sem.at[0], rep_sem.at[1], to)
-        send(cur_all.at[x], cur_all.at[x], rep_sem.at[2], rep_sem.at[3], to)
-
     fill(asked_w.at[pl.ds(0, NW - 1)], w_sem.at[1])
     wanted = jnp.concatenate([asked_w[i] for i in range(NW)] + [jnp.zeros((128 - NW, 128), jnp.int32)], 0)
     asked_t[...] = wanted.T
     wanted = asked_t[pl.ds(0, NY * CAP), :]
     lane = lax.broadcasted_iota(jnp.int32, (NY * CAP, SHARD), 1)
-    for c in range(NW // CHUNK):
-        for q in range(CHUNK):
-            i = c * CHUNK + q
-            hit = jnp.broadcast_to(wanted[:, i : i + 1], (NY * CAP, SHARD)) == lane
+    for c, chunk in enumerate(CHUNKS):
+        first, lists = chunk[0] * CORES, len(chunk) * CORES
+        for q in range(lists):
+            hit = jnp.broadcast_to(wanted[:, first + q : first + q + 1], (NY * CAP, SHARD)) == lane
             onehot[pl.ds(q * NY * CAP, NY * CAP), :] = hit.astype(F32).astype(BF16)
         if c == 0:
             copies[4].wait()
             copies[5].wait()
-        got = dot(onehot[...], hist[...])
-        both = jnp.concatenate(
-            [got[:, :H].reshape(CHUNK * NY, CAP, H), got[:, H:].reshape(CHUNK * NY, CAP, H)], 1
-        )
-        rows_out[pl.ds(c * CHUNK, CHUNK)] = both.astype(BF16).reshape(CHUNK, NY, 2 * CAP, H)
+        got = dot(onehot[pl.ds(0, lists * NY * CAP), :], hist[...])
+        both = jnp.concatenate([got[:, :H].reshape(lists * NY, CAP, H), got[:, H:].reshape(lists * NY, CAP, H)], 1)
+        rows_out[pl.ds(first, lists)] = both.astype(BF16).reshape(lists, NY, 2 * CAP, H)
         for j, ky in STEPS[c]:
             for other in range(CORES):
                 if FAR[j] or ky or other:
@@ -309,12 +309,12 @@
     for k in FAR[:-1]:
         to = (z + k) % NZ * CORES + core
         send(sum_z.at[z], sum_z.at[z], red_sem.at[2], red_sem.at[3], dev(y, to, x))
-    for k in X_ORDER:
-        send(fresh_all.at[x], fresh_all.at[x], rep_sem.at[4], rep_sem.at[5], dev(y, w, (x + k) % NX))
     fill(sum_z.at[pl.ds(0, NZ - 1)], red_sem.at[3])
     sum_y[y] = jnp.sum(sum_z[...].astype(F32), 0).astype(BF16)
     for k in FAR[:-1]:
         send(sum_y.at[y], sum_y.at[y], red_sem.at[4], red_sem.at[5], dev((y + k) % NY, w, x))
+    for k in X_ORDER:
+        send(fresh_all.at[x], fresh_all.at[x], rep_sem.at[4], rep_sem.at[5], dev(y, w, (x + k) % NX))
     fill(sum_y.at[pl.ds(0, NY - 1)], red_sem.at[5])
     total[group] = (jnp.sum(sum_y[...].astype(F32), 0) * SCALE).astype(BF16)
     for _, device in friends:

time: 60.1 us -> 59.9 us (level)
  no operation moved by 1% of the time
where the time goes in v5:
time: 59.9 us; the launch traced here: 59.7 us
  Pallas kernels  59.1 us (99%)
  between operations  0.64 us (1%)
    pallas_call x1, Pallas kernels, on_device(): pl.pallas_call(kernel, name='gcn', out_shape=(sds((BATCH, H), BF16), sds(...  58 us

profile of v5, /device:TPU:1, one launch (start us, length us, event | category | flops | bytes accessed | tf_op | source)
XLA Modules:
  0.0 59.7 jit_solution(15214594439953383568)
XLA Ops:
  0.6 58.0 %gcn.1 = (bf16[256,128]{1,0:T(8,128)(2,1)S(1)}, bf16[2048,128]{1,0:T(8,128)(2,1)S(1)}, bf16[2048,128]{1,0:T(8,128)(2,1)S(1)}, f32[128,128]{1,0:T(8,128)S(1)}, f32[128,128]{1,0:T(8,128)S(1)}) custom-call(s32[8,128]{1,0:T(8,128)} %bitcast.7, s32[1,128]{1,0:T(1,128)} %halo_count.1, s32[1,256]{1,0:T(1,128)} %bitcast.8, s32[2,8]{1,0:T(2,128)} %bitcast.9, ...), custom_call_target="tpu_custom_call" | custom-call | tf_op jit(solution)/shard_map/gcn/pallas_call | solution.py:374
  58.7 1.1 %write_out.1 = (bf16[256,128]{1,0:T(8,128)(2,1)}, bf16[2048,128]{1,0:T(8,128)(2,1)}, bf16[2048,128]{1,0:T(8,128)(2,1)}, f32[128,128]{1,0:T(8,128)}, f32[128,128]{1,0:T(8,128)}) custom-call(bf16[256,128]{1,0:T(8,128)(2,1)S(1)} %get-tuple-element.10.refs_0_, bf16[2048,128]{1,0:T(8,128)(2,1)S(1)} %get-tuple-element.11.refs_1_, ...), custom_call_target="tpu_custom_call" | custom-call | tf_op jit(solution)/shard_map/write_out/pallas_call | solution.py:441

commit v6 on v5

--- a/solution.py
+++ b/solution.py
@@ -45,7 +45,7 @@
 
 def schedule():
     steps, left = [], []
-    for chunk, some in zip(CHUNKS, (8, 4, 6, 6, 64)):
+    for chunk, some in zip(CHUNKS, (8, 0, 0, 0, 64)):
         left = sorted(left + [(j, ky) for j in chunk for ky in FAR], key=hops)
         steps.append(left[:some])
         left = left[some:]

time: 59.9 us -> 59.2 us (0.988)
  Pallas kernels: 59.1 us -> 58.4 us
    pallas_call x1, Pallas kernels: 58 us -> 57.3 us  [on_device(): pl.pallas_call(kernel, name='gcn', out_shape=(sds((BATCH, H), BF16), sds(...]
where the time goes in v6:
time: 59.2 us; the launch traced here: 59 us
  Pallas kernels  58.4 us (99%)
  between operations  0.64 us (1%)
    pallas_call x1, Pallas kernels, on_device(): pl.pallas_call(kernel, name='gcn', out_shape=(sds((BATCH, H), BF16), sds(...  57.3 us

profile of v6, /device:TPU:1, one launch (start us, length us, event | category | flops | bytes accessed | tf_op | source)
XLA Modules:
  0.0 59.0 jit_solution(9260746627922188637)
XLA Ops:
  0.6 57.3 %gcn.1 = (bf16[256,128]{1,0:T(8,128)(2,1)S(1)}, bf16[2048,128]{1,0:T(8,128)(2,1)S(1)}, bf16[2048,128]{1,0:T(8,128)(2,1)S(1)}, f32[128,128]{1,0:T(8,128)S(1)}, f32[128,128]{1,0:T(8,128)S(1)}) custom-call(s32[8,128]{1,0:T(8,128)} %bitcast.7, s32[1,128]{1,0:T(1,128)} %halo_count.1, s32[1,256]{1,0:T(1,128)} %bitcast.8, s32[2,8]{1,0:T(2,128)} %bitcast.9, ...), custom_call_target="tpu_custom_call" | custom-call | tf_op jit(solution)/shard_map/gcn/pallas_call | solution.py:374
  58.0 1.1 %write_out.1 = (bf16[256,128]{1,0:T(8,128)(2,1)}, bf16[2048,128]{1,0:T(8,128)(2,1)}, bf16[2048,128]{1,0:T(8,128)(2,1)}, f32[128,128]{1,0:T(8,128)}, f32[128,128]{1,0:T(8,128)}) custom-call(bf16[256,128]{1,0:T(8,128)(2,1)S(1)} %get-tuple-element.10.refs_0_, bf16[2048,128]{1,0:T(8,128)(2,1)S(1)} %get-tuple-element.11.refs_1_, ...), custom_call_target="tpu_custom_call" | custom-call | tf_op jit(solution)/shard_map/write_out/pallas_call | solution.py:441
